TPU v7x, 32 devices: a whole 2x2x4 slice. The times are simulated.
32 devices in a mesh: parts: 2 (over x), dom: 16 (over z, y, core).
Axes of the slice: x: 2, y: 2, z: 4, core: 2. Of those that a mesh axis runs over, the one named last changes fastest.
Arguments:
- nodes: bfloat16 [8192, 512], P(('parts', 'dom')), parts along dimension 0, may hold values from -6 to 6
- node_count: int32 [32], P(('parts', 'dom')), parts along dimension 0, may hold values from 64 to 256, as said below
- edge_src: int32 [32768], P(('parts', 'dom')), parts along dimension 0, may hold values from 0 to 383, as said below
- edge_dst: int32 [32768], P(('parts', 'dom')), parts along dimension 0, may hold values from 0 to 255, as said below
- edge_count: int32 [32], P(('parts', 'dom')), parts along dimension 0, may hold values from 256 to 1024, as said below
- send_list: int32 [32, 8, 16], P(('parts', 'dom')), parts along dimension 0, may hold values from 0 to 255, as said below
- assign: int32 [8192], P(('parts', 'dom')), parts along dimension 0, may hold values from 0 to 63, as said below
- w_in: bfloat16 [1024, 1024], replicated, may hold values from -0.1875 to 0.1875
- b_in: float32 [1024], replicated, may hold values from -3 to 3
- w_out: bfloat16 [1024, 512], replicated, may hold values from -0.1875 to 0.1875
- w_back: bfloat16 [512, 512], replicated, may hold values from -0.25 to 0.25
- grad_out: bfloat16 [8192, 512], P(('parts', 'dom')), parts along dimension 0, may hold values from -6 to 6
Outputs:
- fields: bfloat16 [8192, 512], P(('parts', 'dom')), parts along dimension 0
- grad_nodes: bfloat16 [8192, 512], P(('parts', 'dom')), parts along dimension 0
- grad_w_in: float32 [2048, 1024], P(('parts', 'dom')), parts along dimension 0
- grad_b_in: float32 [2048], P(('parts', 'dom')), parts along dimension 0
- grad_w_out: float32 [2048, 512], P(('parts', 'dom')), parts along dimension 0
- grad_w_back: float32 [1024, 512], P(('parts', 'dom')), parts along dimension 0
There are 2 independent parts, one for each index of `parts`. A program takes and returns all parts, laid end to end along the dimension named above; an argument that names none is the same for every part. Nothing has to cross between parts.
Inputs may be any that keep to these rules, and one draw needn't show every extreme that they name: `node_count`: one partition is full in every draw. `edge_count`: one partition is full in every draw. `edge_dst`: below the node count of the edge's partition. `edge_src`: a value under 256 is a row of the edge's own partition below its node count; a larger one is 256 + 16 * k + s, slot s of the rows that the partition's neighbour in direction k sends it, and that neighbour lies on the grid. send_list[j, k, s] is below the node count of partition j. `assign`: a fine node of partition p is assigned a coarse node of (p - 1) * 4 to (p + 2) * 4 - 1, taken modulo 64.
All inputs are finite; a program needn't handle non-finite values.
Results may differ from a plain program's by a relative error of at most 0.008.
Values may be sent and summed in bfloat16 or wider, within the bound.
A program may use at most 64 MiB of HBM per device.

v0:
```python
import jax
import jax.numpy as jnp
from jax import lax
from jax.sharding import PartitionSpec as P

GRID_Y = 8
CO_DEV = 4


directions = ((-1, -1), (-1, 0), (-1, 1), (0, -1), (0, 1), (1, -1), (1, 0), (1, 1))


def from_behind(value, axis, steps):
    count = lax.axis_size(axis)
    initial, last = (max(0, -steps), min(count, count - steps))
    return lax.ppermute(value, axis, [(source, source + steps) for source in range(initial, last)])


def passed_along(block, axis, distance):
    devices = range(lax.axis_size(axis))
    route = [((i - distance) % len(devices), i) for i in devices]
    return lax.ppermute(block, axis, route)


def direction_index(row_step, col_step):
    return directions.index((row_step, col_step))


def silu_grad(argument):
    squashed = jax.nn.sigmoid(argument)
    return squashed * (1.0 + argument * (1.0 - squashed))


def contract_rows(left_side, right_side):
    return lax.dot_general(
        left_side, right_side, (((0,), (0,)), ((), ())), preferred_element_type=jnp.float32
    )


def contract_cols(left_side, right_side):
    return lax.dot_general(
        left_side, right_side, (((1,), (1,)), ((), ())), preferred_element_type=jnp.float32
    )


def plain_dot(left_side, right_side):
    return jnp.dot(left_side, right_side, preferred_element_type=jnp.float32)


def exact_sum(hot_table, values, product):
    upper_part = values.astype(jnp.bfloat16)
    lower_part = (values - upper_part.astype(jnp.float32)).astype(jnp.bfloat16)
    return product(hot_table, upper_part) + product(hot_table, lower_part)


def route_sectioned(blocks, move_across, move_along):
    received = {}
    carried = []
    for row_step in (-1, 1):
        payload = jnp.stack(
            [
                blocks[direction_index(row_step, -1)],
                blocks[direction_index(row_step, 0)],
                blocks[direction_index(row_step, 1)],
            ]
        )
        arrived = move_across(payload, row_step * GRID_Y)
        received[direction_index(-row_step, 0)] = arrived[1]
        carried.append(arrived)
    for col_step in (-1, 1):
        chosen = 0 if col_step < 0 else 2
        payload = jnp.stack(
            [blocks[direction_index(0, col_step)], carried[0][chosen], carried[1][chosen]]
        )
        arrived = move_along(payload, col_step)
        received[direction_index(0, -col_step)] = arrived[0]
        received[direction_index(1, -col_step)] = arrived[1]
        received[direction_index(-1, -col_step)] = arrived[2]
    return [received[ordinal] for ordinal in range(len(directions))]


def body(
    nodes,
    node_count,
    edge_src,
    edge_dst,
    edge_count,
    send_list,
    assign,
    w_in,
    b_in,
    w_out,
    w_back,
    grad_out,
):
    num_nodes, latent = nodes.shape
    num_edges = edge_src.shape[0]
    parties = lax.axis_size("dom")
    coarse_total = CO_DEV * parties
    window = 3 * CO_DEV
    count_dirs = len(directions)
    valid_bool = jnp.arange(num_nodes) < node_count[0]
    valid_rows = valid_bool.astype(jnp.float32)[:, None]
    first_state = (nodes.astype(jnp.float32) * valid_rows).astype(jnp.bfloat16)
    send_rows = send_list[0].reshape(-1)
    outgoing = jnp.take(first_state, send_rows, axis=0).reshape(count_dirs, -1, latent)

    def send_across(payload, offset):
        return from_behind(payload, "dom", offset)

    def send_along(payload, offset):
        return from_behind(payload, "dom", offset)

    arrived = route_sectioned(outgoing, send_across, send_along)
    node_table = jnp.concatenate([first_state] + arrived, axis=0)
    src_rows = jnp.take(node_table, edge_src, axis=0)
    dst_rows = jnp.take(first_state, edge_dst, axis=0)
    weight_src = w_in[:latent]
    weight_dst = w_in[latent:]
    preact = (
        jnp.dot(src_rows, weight_src, preferred_element_type=jnp.float32)
        + jnp.dot(dst_rows, weight_dst, preferred_element_type=jnp.float32)
        + b_in
    )
    hidden = jax.nn.silu(preact).astype(jnp.bfloat16)
    edge_mask = (jnp.arange(num_edges) < edge_count[0]).astype(jnp.float32)[:, None]
    message = (jnp.dot(hidden, w_out, preferred_element_type=jnp.float32) * edge_mask).astype(
        jnp.bfloat16
    )
    dst_hot = (edge_dst[:, None] == jnp.arange(num_nodes)[None, :]).astype(jnp.bfloat16)
    summed = contract_rows(dst_hot, message)
    mid_state = ((first_state.astype(jnp.float32) + summed) * valid_rows).astype(jnp.bfloat16)
    position = lax.axis_index("dom")
    window_ids = (position * CO_DEV - CO_DEV + jnp.arange(window)) % coarse_total
    coarse_hot = ((window_ids[:, None] == assign[None, :]) & valid_bool[None, :]).astype(
        jnp.bfloat16
    )
    pooled = plain_dot(coarse_hot, mid_state)
    counts = jnp.sum(coarse_hot.astype(jnp.float32), axis=1)
    own_sum = pooled[CO_DEV : 2 * CO_DEV]
    own_count = counts[CO_DEV : 2 * CO_DEV]
    for offset, side_sum, side_count in (
        (1, pooled[2 * CO_DEV :], counts[2 * CO_DEV :]),
        (-1, pooled[:CO_DEV], counts[:CO_DEV]),
    ):
        moved_sum, moved_count = passed_along((side_sum, side_count), "dom", offset)
        own_sum = own_sum + moved_sum
        own_count = own_count + moved_count
    inverse_own = 1.0 / jnp.maximum(own_count, 1.0)
    coarse_own = (own_sum * inverse_own[:, None]).astype(jnp.bfloat16)
    beside = [passed_along(coarse_own, "dom", offset) for offset in (1, -1)]
    coarse_win = jnp.concatenate([beside[0], coarse_own, beside[1]], axis=0)
    spread = contract_rows(coarse_hot, coarse_win)
    lifted = jax.nn.silu(spread).astype(jnp.bfloat16)
    fields = (
        (
            mid_state.astype(jnp.float32)
            + jnp.dot(lifted, w_back, preferred_element_type=jnp.float32)
        )
        * valid_rows
    ).astype(jnp.bfloat16)
    grad_top = (grad_out.astype(jnp.float32) * valid_rows).astype(jnp.bfloat16)
    grad_back = contract_rows(lifted, grad_top)
    grad_spread = contract_cols(grad_top, w_back) * silu_grad(spread)
    grad_pool = exact_sum(coarse_hot, grad_spread, plain_dot)
    grad_own = grad_pool[CO_DEV : 2 * CO_DEV]
    for offset, side_grad in ((1, grad_pool[2 * CO_DEV :]), (-1, grad_pool[:CO_DEV])):
        grad_own = grad_own + passed_along(side_grad, "dom", offset)
    grad_own = grad_own * inverse_own[:, None]
    beside_grad = [passed_along(grad_own, "dom", offset) for offset in (1, -1)]
    grad_win = jnp.concatenate([beside_grad[0], grad_own, beside_grad[1]], axis=0)
    lifted_grad = exact_sum(coarse_hot, grad_win, contract_rows)
    grad_mid = ((grad_top.astype(jnp.float32) + lifted_grad) * valid_rows).astype(jnp.bfloat16)
    grad_msg = (jnp.take(grad_mid, edge_dst, axis=0).astype(jnp.float32) * edge_mask).astype(
        jnp.bfloat16
    )
    grad_pre = (contract_cols(grad_msg, w_out) * silu_grad(preact)).astype(jnp.bfloat16)
    grad_wout = contract_rows(hidden, grad_msg)
    grad_weight_in = jnp.concatenate(
        [contract_rows(src_rows, grad_pre), contract_rows(dst_rows, grad_pre)], axis=0
    )
    grad_bias = jnp.sum(grad_pre.astype(jnp.float32), axis=0)
    grad_xsrc = contract_cols(grad_pre, weight_src)
    grad_xdst = contract_cols(grad_pre, weight_dst)
    src_hot = (edge_src[:, None] == jnp.arange(node_table.shape[0])[None, :]).astype(jnp.bfloat16)
    grad_table = exact_sum(src_hot, grad_xsrc, contract_rows)
    grad_local = exact_sum(dst_hot, grad_xdst, contract_rows)
    halo_part = grad_table[num_nodes:].reshape(count_dirs, -1, latent)

    def return_across(payload, offset):
        return from_behind(payload.astype(jnp.bfloat16), "dom", offset).astype(payload.dtype)

    def return_along(payload, offset):
        return from_behind(payload.astype(jnp.bfloat16), "dom", offset).astype(payload.dtype)

    back_blocks = route_sectioned(halo_part, return_across, return_along)
    returned = jnp.concatenate(back_blocks, axis=0)
    owner_hot = (send_rows[:, None] == jnp.arange(num_nodes)[None, :]).astype(jnp.bfloat16)
    grad_owned = exact_sum(owner_hot, returned, contract_rows)
    grad_total = grad_mid.astype(jnp.float32) + grad_table[:num_nodes] + grad_local + grad_owned
    grad_nodes = (grad_total * valid_rows).astype(jnp.bfloat16)
    reduced = (
        lax.psum_scatter(grad_weight_in, "dom", scatter_dimension=0, tiled=True),
        lax.psum_scatter(grad_bias, "dom", scatter_dimension=0, tiled=True),
        lax.psum_scatter(grad_wout, "dom", scatter_dimension=0, tiled=True),
        lax.psum_scatter(grad_back, "dom", scatter_dimension=0, tiled=True),
    )
    return (fields, grad_nodes, reduced[0], reduced[1], reduced[2], reduced[3])


def solution(mesh):
    return jax.shard_map(
        body,
        mesh=mesh,
        in_specs=(
            P(("parts", "dom"), None),
            P(("parts", "dom")),
            P(("parts", "dom")),
            P(("parts", "dom")),
            P(("parts", "dom")),
            P(("parts", "dom"), None, None),
            P(("parts", "dom")),
            P(),
            P(),
            P(),
            P(),
            P(("parts", "dom"), None),
        ),
        out_specs=(
            P(("parts", "dom"), None),
            P(("parts", "dom"), None),
            P(("parts", "dom"), None),
            P(("parts", "dom")),
            P(("parts", "dom"), None),
            P(("parts", "dom"), None),
        ),
        check_vma=False,
    )
```

profile of v0, /device:TPU:0, one launch (start us, length us, event | category | flops | bytes accessed | tf_op | source)
XLA Modules:
  0.0 272.4 jit_solution(2043353372272041935)
XLA Ops:
  8.0 0.9 convert_reduce_fusion.1
  9.4 5.0 %collective-permute-start.7 = (f32[4]{0:T(128)S(1)}, f32[4]{0:T(128)S(1)}, u32[]{:S(2)}, u32[]{:S(2)}) collective-permute-start(f32[4]{0:T(128)S(1)} %get-tuple-element.38), channel_id=1, source_target_pairs={{1,0},{2,1},{3,2},{4,3},{5,4},{6,5},{7,6},{8,7},{9,8},{10,9},{11,1... | collective-permute-start | bytes 56 | tf_op jit(solution)/shard_map/ppermute | solution.py:22
  16.0 1.1 constant_dynamic-update-slice_fusion.8
  17.1 0.8 gather_fusion
  18.1 1.3 collective-permute-start
  19.4 5.4 %collective-permute-start.1 = (bf16[3,16,512]{2,1,0:T(8,128)(2,1)S(1)}, bf16[3,16,512]{2,1,0:T(8,128)(2,1)S(1)}, u32[]{:S(2)}, u32[]{:S(2)}) collective-permute-start(bf16[3,16,512]{2,1,0:T(8,128)(2,1)S(1)} %pad_maximum_fusion.2), channel_id=1, source_target_pairs={{0,8},{1,9},{2,10},{3,11},{4,12},{5,13},{6,14},{7,15},{16,24},{17,... | collective-permute-start | bytes 147464 | tf_op jit(solution)/shard_map/ppermute | solution.py:16
  25.6 4.0 %gather_fusion.2 = bf16[1024,512]{1,0:T(8,128)(2,1)S(1)} fusion(bf16[256,512]{1,0:T(8,128)(2,1)S(1)} %get-tuple-element.8, s32[1024]{0:T(1024)S(1)} %fusion.78), kind=kCustom, calls=%fused_computation.clone | custom fusion | bytes 2101248 | tf_op jit(solution)/shard_map/jit(_take)/gather | solution.py:117
  29.6 1.3 collective-permute-start.2
  30.9 1.3 collective-permute-start.3
  32.3 1.8 collective-permute-done.3
  34.1 5.1 %gather_fusion.1 = bf16[1024,512]{1,0:T(8,128)(2,1)} fusion(bf16[384,512]{1,0:T(8,128)(2,1)S(1)} %constant_dynamic-update-slice_fusion, s32[1024]{0:T(1024)S(1)} %fusion.77), kind=kCustom, calls=%fused_computation.3 | custom fusion | bytes 2101248 | tf_op jit(solution)/shard_map/jit(_take)/gather | solution.py:116
  39.2 3.0 %fusion.20 = f32[1024,1024]{1,0:T(8,128)S(1)} fusion(bf16[1024,1024]{1,0:T(8,128)(2,1)} %param.21, bf16[1024,512]{1,0:T(8,128)(2,1)} %gather_fusion.1, pred[1024]{0:T(1024)(128)(4,1)S(1)} %compare_and_fusion.8), kind=kOutput, calls=%fused_computation.45 | convolution fusion | flops 1074266112 | bytes 6292480 | tf_op jit(solution)/shard_map/dot_general | solution.py:121
  42.2 4.3 %multiply_convert_fusion.1 = (bf16[1024,1024]{1,0:T(8,128)(2,1)}, f32[1024,1024]{1,0:T(8,128)}) fusion(f32[1024]{0:T(1024)S(1)} %copy-done.17, f32[1024,1024]{1,0:T(8,128)S(1)} %fusion.20, bf16[1024,1024]{1,0:T(8,128)(2,1)S(1)} %copy-done.15, bf16[1024,512]{1,0:T(8,128)(2,1)S(1)} %gather_fusion.2, pred[1024]{0:T(1024)(128)(4,1)S(1)} %compare_and_fusion.7), kind=kOutput, calls=%fused_computation.7 | convolution fusion | flops 1081606144 | bytes 12588032 | tf_op jit(solution)/shard_map/dot_general | solution.py:122
  46.5 3.2 %fusion.13 = bf16[256,512]{1,0:T(8,128)(2,1)S(1)} fusion(bf16[1024,1024]{1,0:T(8,128)(2,1)} %get-tuple-element.39, bf16[1024,512]{1,0:T(8,128)(2,1)S(1)} %copy-done, f32[1024]{0:T(1024)S(1)} %fusion.76, s32[1024]{0:T(1024)S(1)} %copy-done.12, bf16[256,512]{1,0:T(8,128)(2,1)S(1)} %get-tuple-element.8, f32[256]{0:T(256)S(1)} %get-tuple-element.46), kind=kOutput, calls=%fused_computation.34 | convolution fusion | flops 1344012288 | bytes 3679232 | tf_op jit(solution)/shard_map/dot_general | solution.py:35
  49.9 2.2 collective-permute-start.4
  52.1 2.2 collective-permute-start.5
  54.4 1.2 collective-permute-done.4
  55.7 4.4 %collective-permute-start.9 = (bf16[4,512]{1,0:T(4,128)(2,1)S(1)}, bf16[4,512]{1,0:T(4,128)(2,1)S(1)}, u32[]{:S(2)}, u32[]{:S(2)}) collective-permute-start(bf16[4,512]{1,0:T(4,128)(2,1)S(1)} %fusion.57), channel_id=1, source_target_pairs={{1,0},{2,1},{3,2},{4,3},{5,4},{6,5},{7,6},{8,7},{9,8},{10,9},{11,1... | collective-permute-start | bytes 12296 | tf_op jit(solution)/shard_map/ppermute | solution.py:22
  60.2 1.3 collective-permute-done.9
  61.5 4.4 %collective-permute-done.8 = bf16[4,512]{1,0:T(4,128)(2,1)S(1)} collective-permute-done((bf16[4,512]{1,0:T(4,128)(2,1)S(1)}, bf16[4,512]{1,0:T(4,128)(2,1)S(1)}, u32[]{:S(2)}, u32[]{:S(2)}) %collective-permute-start.8) | collective-permute-done | bytes 4128 | tf_op jit(solution)/shard_map/ppermute | solution.py:22
  66.2 1.4 fusion.89
  67.6 1.4 convolution_multiply_fusion
  69.5 4.4 %collective-permute-start.11 = (f32[4,512]{1,0:T(4,128)S(1)}, f32[4,512]{1,0:T(4,128)S(1)}, u32[]{:S(2)}, u32[]{:S(2)}) collective-permute-start(f32[4,512]{1,0:T(4,128)S(1)} %get-tuple-element.34), channel_id=1, source_target_pairs={{1,0},{2,1},{3,2},{4,3},{5,4},{6,5},{7,6},{8,7},{9,8},{10,9},{11,1... | collective-permute-start | bytes 24584 | tf_op jit(solution)/shard_map/ppermute | solution.py:22
  74.0 1.3 collective-permute-done.10
  75.4 4.4 %collective-permute-start.13 = (f32[4,512]{1,0:T(4,128)S(1)}, f32[4,512]{1,0:T(4,128)S(1)}, u32[]{:S(2)}, u32[]{:S(2)}) collective-permute-start(f32[4,512]{1,0:T(4,128)S(1)} %fusion.54), channel_id=1, source_target_pairs={{1,0},{2,1},{3,2},{4,3},{5,4},{6,5},{7,6},{8,7},{9,8},{10,9},{11,1... | collective-permute-start | bytes 24584 | tf_op jit(solution)/shard_map/ppermute | solution.py:22
  79.8 1.4 collective-permute-done.13
  81.2 4.4 %collective-permute-done.12 = f32[4,512]{1,0:T(4,128)S(1)} collective-permute-done((f32[4,512]{1,0:T(4,128)S(1)}, f32[4,512]{1,0:T(4,128)S(1)}, u32[]{:S(2)}, u32[]{:S(2)}) %collective-permute-start.12) | collective-permute-done | bytes 8224 | tf_op jit(solution)/shard_map/ppermute | solution.py:22
  86.3 4.0 %gather_fusion.3 = bf16[1024,512]{1,0:T(8,128)(2,1)S(1)} fusion(bf16[256,512]{1,0:T(8,128)(2,1)S(1)} %fusion.12, s32[1024]{0:T(1024)S(1)} %fusion.78), kind=kCustom, calls=%fused_computation.1.clone | custom fusion | bytes 2101248 | tf_op jit(solution)/shard_map/jit(_take)/gather | solution.py:174
  90.3 4.7 %fusion.90 = f32[1024,512]{1,0:T(8,128)} fusion(bf16[1024,1024]{1,0:T(8,128)(2,1)} %get-tuple-element.39, bf16[1024,512]{1,0:T(8,128)(2,1)S(1)} %gather_fusion.3, f32[1024]{0:T(1024)S(1)} %fusion.76, pred[1024]{0:T(1024)(128)(4,1)S(1)} %compare_and_fusion.7), kind=kOutput, calls=%fused_computation.199 | convolution fusion | flops 1075838976 | bytes 5248000 | tf_op jit(solution)/shard_map/dot_general | solution.py:35
  95.3 4.8 %convert_reduce_fusion = (f32[1024]{0:T(1024)S(1)}, bf16[1024,1024]{1,0:T(8,128)(2,1)S(1)}) fusion(f32[1024,1024]{1,0:T(8,128)} %get-tuple-element.40, bf16[1024,512]{1,0:T(8,128)(2,1)S(1)} %copy-done, bf16[1024,512]{1,0:T(8,128)(2,1)} %copy-done.8, f32[1024]{0:T(1024)S(1)} %fusion.76, pred[1024]{0:T(1024)(128)(4,1)S(1)} %compare_and_fusion.7), kind=kOutput, calls=%fused_computation.5 | convolution fusion | flops 1087372288 | bytes 8397824 | tf_op jit(solution)/shard_map/dot_general | solution.py:41
  100.1 1.4 fusion.32
  102.1 1.4 fusion.31
  103.4 2.5 pad_maximum_fusion
  107.9 2.5 fusion.10
  110.3 1.3 fusion.18
  111.6 0.9 fusion
  112.6 1.9 fusion.98
  114.5 1.3 collective-permute-start.14
  115.8 1.3 fusion.15
  117.1 5.4 %collective-permute-start.15 = (bf16[3,16,512]{2,1,0:T(8,128)(2,1)S(1)}, bf16[3,16,512]{2,1,0:T(8,128)(2,1)S(1)}, u32[]{:S(2)}, u32[]{:S(2)}) collective-permute-start(bf16[3,16,512]{2,1,0:T(8,128)(2,1)S(1)} %pad_maximum_fusion.6), channel_id=1, source_target_pairs={{0,8},{1,9},{2,10},{3,11},{4,12},{5,13},{6,14},{7,15},{16,24},{17,... | collective-permute-start | bytes 147464 | tf_op jit(solution)/shard_map/ppermute | solution.py:16
  122.6 1.7 collective-permute-done.15
  124.9 1.9 collective-permute-start.16
  127.4 1.3 collective-permute-start.17
  128.7 1.5 fusion.14
  130.2 30.8 %all-reduce = f32[1024]{0:T(1024)S(1)} all-reduce(f32[1024]{0:T(1024)S(1)} %get-tuple-element.43), channel_id=3, replica_groups=mesh['parts'=2,'dom'=16] {'dom'}, use_global_device_ids=true, to_apply=%region_3.5.clone | all-reduce | flops 1024 | bytes 8192
  164.0 1.4 fusion.11
  165.5 24.5 %reduce-scatter.6.cloned.1.call-done = f32[64,512]{1,0:T(8,128)} async-done(((f32[1024,512]{1,0:T(8,128)}), f32[64,512]{1,0:T(8,128)}) %reduce-scatter.6.cloned.1.call-update) | async-done | bytes 131088 | tf_op jit(solution)/shard_map/reduce_scatter | solution.py:205
  190.0 75.9 %reduce-scatter.4.cloned.1.call-done = f32[64,1024]{1,0:T(8,128)} async-done(((f32[1024,1024]{1,0:T(8,128)}), f32[64,1024]{1,0:T(8,128)}) %reduce-scatter.4.cloned.1.call-update) | async-done | bytes 262160 | tf_op jit(solution)/shard_map/reduce_scatter | solution.py:203
  (120 shorter events, 10.7 us)
Async XLA Ops:
  7.2 39.3 %copy-start = (bf16[1024,512]{1,0:T(8,128)(2,1)S(1)}, bf16[1024,512]{1,0:T(8,128)(2,1)}, u32[]{:S(2)}) copy-start(bf16[1024,512]{1,0:T(8,128)(2,1)} %param.23) | copy-start | bytes 3145732
  7.2 17.6 %copy-start.12 = (s32[1024]{0:T(1024)S(1)}, s32[1024]{0:T(1024)}, u32[]{:S(2)}) copy-start(s32[1024]{0:T(1024)} %param.17) | copy-start | bytes 12292
  7.2 17.7 %copy-start.14 = (s32[1024]{0:T(1024)S(1)}, s32[1024]{0:T(1024)}, u32[]{:S(2)}) copy-start(s32[1024]{0:T(1024)} %param.16) | copy-start | bytes 12292
  7.2 158.3 %reduce-scatter.8.cloned.1.call-start = ((), (), s32[]{:S(2)}) async-start(), calls=%async_computation.5 | async-start | bytes 1114112 | tf_op jit(solution)/shard_map/reduce_scatter | solution.py:206
  8.9 45.4 %collective-permute-start.6 = (f32[4]{0:T(128)S(1)}, f32[4]{0:T(128)S(1)}, u32[]{:S(2)}, u32[]{:S(2)}) collective-permute-start(f32[4]{0:T(128)S(1)} %get-tuple-element.37), channel_id=1, source_target_pairs={{15,0},{0,1},{1,2},{2,3},{3,4},{4,5},{5,6},{6,7},{7,8},{8,9},{9,10... | collective-permute-start | bytes 56 | tf_op jit(solution)/shard_map/ppermute | solution.py:22
  9.4 44.9 %collective-permute-start.7 = (f32[4]{0:T(128)S(1)}, f32[4]{0:T(128)S(1)}, u32[]{:S(2)}, u32[]{:S(2)}) collective-permute-start(f32[4]{0:T(128)S(1)} %get-tuple-element.38), channel_id=1, source_target_pairs={{1,0},{2,1},{3,2},{4,3},{5,4},{6,5},{7,6},{8,7},{9,8},{10,9},{11,1... | collective-permute-start | bytes 56 | tf_op jit(solution)/shard_map/ppermute | solution.py:22
  18.1 11.5 %collective-permute-start = (bf16[3,16,512]{2,1,0:T(8,128)(2,1)S(1)}, bf16[3,16,512]{2,1,0:T(8,128)(2,1)S(1)}, u32[]{:S(2)}, u32[]{:S(2)}) collective-permute-start(bf16[3,16,512]{2,1,0:T(8,128)(2,1)S(1)} %pad_maximum_fusion.1), channel_id=1, source_target_pairs={{8,0},{9,1},{10,2},{11,3},{12,4},{13,5},{14,6},{15,7},{24,16},{25,... | collective-permute-start | bytes 147464 | tf_op jit(solution)/shard_map/ppermute | solution.py:16
  19.4 10.2 %collective-permute-start.1 = (bf16[3,16,512]{2,1,0:T(8,128)(2,1)S(1)}, bf16[3,16,512]{2,1,0:T(8,128)(2,1)S(1)}, u32[]{:S(2)}, u32[]{:S(2)}) collective-permute-start(bf16[3,16,512]{2,1,0:T(8,128)(2,1)S(1)} %pad_maximum_fusion.2), channel_id=1, source_target_pairs={{0,8},{1,9},{2,10},{3,11},{4,12},{5,13},{6,14},{7,15},{16,24},{17,... | collective-permute-start | bytes 147464 | tf_op jit(solution)/shard_map/ppermute | solution.py:16
  29.5 12.7 %copy-start.3 = (bf16[1024,512]{1,0:T(8,128)(2,1)}, bf16[1024,512]{1,0:T(8,128)(2,1)S(1)}, u32[]{:S(2)}) copy-start(bf16[1024,512]{1,0:T(8,128)(2,1)S(1)} %gather_fusion.2) | copy-start | bytes 3145732
  29.6 2.6 collective-permute-start.2
  30.9 3.1 %collective-permute-start.3 = (bf16[3,16,512]{2,1,0:T(8,128)(2,1)S(1)}, bf16[3,16,512]{2,1,0:T(8,128)(2,1)S(1)}, u32[]{:S(2)}, u32[]{:S(2)}) collective-permute-start(bf16[3,16,512]{2,1,0:T(8,128)(2,1)S(1)} %pad_maximum_fusion.4), channel_id=1, source_target_pairs={{1,0},{2,1},{3,2},{4,3},{5,4},{6,5},{7,6},{8,7},{9,8},{10,9},{11,1... | collective-permute-start | bytes 147464 | tf_op jit(solution)/shard_map/ppermute | solution.py:16
  39.2 3.0 %copy-start.15 = (bf16[1024,1024]{1,0:T(8,128)(2,1)S(1)}, bf16[1024,1024]{1,0:T(8,128)(2,1)}, u32[]{:S(2)}) copy-start(bf16[1024,1024]{1,0:T(8,128)(2,1)} %param.21) | copy-start | bytes 6291460
  39.2 3.0 %copy-start.17 = (f32[1024]{0:T(1024)S(1)}, f32[1024]{0:T(1024)}, u32[]{:S(2)}) copy-start(f32[1024]{0:T(1024)} %param.22) | copy-start | bytes 12292
  46.5 3.2 %copy-start.13 = (s32[256]{0:T(256)S(1)}, s32[256]{0:T(256)}, u32[]{:S(2)}) copy-start(s32[256]{0:T(256)} %param.20) | copy-start | bytes 3076
  46.5 19.8 %copy-start.10 = (bf16[256,512]{1,0:T(8,128)(2,1)S(1)}, bf16[256,512]{1,0:T(8,128)(2,1)}, u32[]{:S(2)}) copy-start(bf16[256,512]{1,0:T(8,128)(2,1)} %param.25) | copy-start | bytes 786436
  49.6 18.0 %copy-start.11 = (bf16[256,512]{1,0:T(8,128)(2,1)}, bf16[256,512]{1,0:T(8,128)(2,1)S(1)}, u32[]{:S(2)}) copy-start(bf16[256,512]{1,0:T(8,128)(2,1)S(1)} %fusion.13) | copy-start | bytes 786436
  49.9 5.8 %collective-permute-start.4 = (f32[4,512]{1,0:T(4,128)S(1)}, f32[4,512]{1,0:T(4,128)S(1)}, u32[]{:S(2)}, u32[]{:S(2)}) collective-permute-start(f32[4,512]{1,0:T(4,128)S(1)} %get-tuple-element.35), channel_id=1, source_target_pairs={{15,0},{0,1},{1,2},{2,3},{3,4},{4,5},{5,6},{6,7},{7,8},{8,9},{9,10... | collective-permute-start | bytes 24584 | tf_op jit(solution)/shard_map/ppermute | solution.py:22
  52.1 3.6 %collective-permute-start.5 = (f32[4,512]{1,0:T(4,128)S(1)}, f32[4,512]{1,0:T(4,128)S(1)}, u32[]{:S(2)}, u32[]{:S(2)}) collective-permute-start(f32[4,512]{1,0:T(4,128)S(1)} %get-tuple-element.36), channel_id=1, source_target_pairs={{1,0},{2,1},{3,2},{4,3},{5,4},{6,5},{7,6},{8,7},{9,8},{10,9},{11,1... | collective-permute-start | bytes 24584 | tf_op jit(solution)/shard_map/ppermute | solution.py:22
  55.7 5.7 %collective-permute-start.9 = (bf16[4,512]{1,0:T(4,128)(2,1)S(1)}, bf16[4,512]{1,0:T(4,128)(2,1)S(1)}, u32[]{:S(2)}, u32[]{:S(2)}) collective-permute-start(bf16[4,512]{1,0:T(4,128)(2,1)S(1)} %fusion.57), channel_id=1, source_target_pairs={{1,0},{2,1},{3,2},{4,3},{5,4},{6,5},{7,6},{8,7},{9,8},{10,9},{11,1... | collective-permute-start | bytes 12296 | tf_op jit(solution)/shard_map/ppermute | solution.py:22
  60.1 5.7 %collective-permute-start.8 = (bf16[4,512]{1,0:T(4,128)(2,1)S(1)}, bf16[4,512]{1,0:T(4,128)(2,1)S(1)}, u32[]{:S(2)}, u32[]{:S(2)}) collective-permute-start(bf16[4,512]{1,0:T(4,128)(2,1)S(1)} %fusion.57), channel_id=1, source_target_pairs={{15,0},{0,1},{1,2},{2,3},{3,4},{4,5},{5,6},{6,7},{7,8},{8,9},{9,10... | collective-permute-start | bytes 12296 | tf_op jit(solution)/shard_map/ppermute | solution.py:22
  66.2 2.8 %copy-start.9 = (f32[256,512]{1,0:T(8,128)}, f32[256,512]{1,0:T(8,128)S(1)}, u32[]{:S(2)}) copy-start(f32[256,512]{1,0:T(8,128)S(1)} %fusion.43) | copy-start | bytes 1572868
  69.3 120.7 %reduce-scatter.6.cloned.1.call-start = ((), (), s32[]{:S(2)}) async-start(), calls=%async_computation.4 | async-start | bytes 2228224 | tf_op jit(solution)/shard_map/reduce_scatter | solution.py:205
  69.5 5.8 %collective-permute-start.10 = (f32[4,512]{1,0:T(4,128)S(1)}, f32[4,512]{1,0:T(4,128)S(1)}, u32[]{:S(2)}, u32[]{:S(2)}) collective-permute-start(f32[4,512]{1,0:T(4,128)S(1)} %get-tuple-element.33), channel_id=1, source_target_pairs={{15,0},{0,1},{1,2},{2,3},{3,4},{4,5},{5,6},{6,7},{7,8},{8,9},{9,10... | collective-permute-start | bytes 24584 | tf_op jit(solution)/shard_map/ppermute | solution.py:22
  69.5 5.8 %collective-permute-start.11 = (f32[4,512]{1,0:T(4,128)S(1)}, f32[4,512]{1,0:T(4,128)S(1)}, u32[]{:S(2)}, u32[]{:S(2)}) collective-permute-start(f32[4,512]{1,0:T(4,128)S(1)} %get-tuple-element.34), channel_id=1, source_target_pairs={{1,0},{2,1},{3,2},{4,3},{5,4},{6,5},{7,6},{8,7},{9,8},{10,9},{11,1... | collective-permute-start | bytes 24584 | tf_op jit(solution)/shard_map/ppermute | solution.py:22
  75.4 5.8 %collective-permute-start.13 = (f32[4,512]{1,0:T(4,128)S(1)}, f32[4,512]{1,0:T(4,128)S(1)}, u32[]{:S(2)}, u32[]{:S(2)}) collective-permute-start(f32[4,512]{1,0:T(4,128)S(1)} %fusion.54), channel_id=1, source_target_pairs={{1,0},{2,1},{3,2},{4,3},{5,4},{6,5},{7,6},{8,7},{9,8},{10,9},{11,1... | collective-permute-start | bytes 24584 | tf_op jit(solution)/shard_map/ppermute | solution.py:22
  79.8 5.8 %collective-permute-start.12 = (f32[4,512]{1,0:T(4,128)S(1)}, f32[4,512]{1,0:T(4,128)S(1)}, u32[]{:S(2)}, u32[]{:S(2)}) collective-permute-start(f32[4,512]{1,0:T(4,128)S(1)} %fusion.54), channel_id=1, source_target_pairs={{15,0},{0,1},{1,2},{2,3},{3,4},{4,5},{5,6},{6,7},{7,8},{8,9},{9,10... | collective-permute-start | bytes 24584 | tf_op jit(solution)/shard_map/ppermute | solution.py:22
  90.3 4.7 %copy-start.8 = (bf16[1024,512]{1,0:T(8,128)(2,1)}, bf16[1024,512]{1,0:T(8,128)(2,1)S(1)}, u32[]{:S(2)}) copy-start(bf16[1024,512]{1,0:T(8,128)(2,1)S(1)} %gather_fusion.3) | copy-start | bytes 3145732
  95.0 170.8 %reduce-scatter.4.cloned.1.call-start = ((), (), s32[]{:S(2)}) async-start(), calls=%async_computation.3 | async-start | bytes 4456448 | tf_op jit(solution)/shard_map/reduce_scatter | solution.py:203
  95.3 4.8 %copy-start.4 = (bf16[1024,512]{1,0:T(8,128)(2,1)S(1)}, bf16[1024,512]{1,0:T(8,128)(2,1)}, u32[]{:S(2)}) copy-start(bf16[1024,512]{1,0:T(8,128)(2,1)} %copy-done.3) | copy-start | bytes 3145732
  100.1 10.3 %copy-start.1 = (bf16[1024,1024]{1,0:T(8,128)(2,1)}, bf16[1024,1024]{1,0:T(8,128)(2,1)S(1)}, u32[]{:S(2)}) copy-start(bf16[1024,1024]{1,0:T(8,128)(2,1)S(1)} %get-tuple-element.44) | copy-start | bytes 6291460
  100.1 2.0 copy-start.5
  106.0 0.7 copy-start.18
  107.9 2.5 copy-start.16
  112.6 3.2 %copy-start.2 = (bf16[1024,1024]{1,0:T(8,128)(2,1)S(1)}, bf16[1024,1024]{1,0:T(8,128)(2,1)}, u32[]{:S(2)}) copy-start(bf16[1024,1024]{1,0:T(8,128)(2,1)} %copy-done.1) | copy-start | bytes 6291460
  114.5 8.1 %collective-permute-start.14 = (bf16[3,16,512]{2,1,0:T(8,128)(2,1)S(1)}, bf16[3,16,512]{2,1,0:T(8,128)(2,1)S(1)}, u32[]{:S(2)}, u32[]{:S(2)}) collective-permute-start(bf16[3,16,512]{2,1,0:T(8,128)(2,1)S(1)} %pad_maximum_fusion.5), channel_id=1, source_target_pairs={{8,0},{9,1},{10,2},{11,3},{12,4},{13,5},{14,6},{15,7},{24,16},{25,... | collective-permute-start | bytes 147464 | tf_op jit(solution)/shard_map/ppermute | solution.py:16
  117.1 7.2 %collective-permute-start.15 = (bf16[3,16,512]{2,1,0:T(8,128)(2,1)S(1)}, bf16[3,16,512]{2,1,0:T(8,128)(2,1)S(1)}, u32[]{:S(2)}, u32[]{:S(2)}) collective-permute-start(bf16[3,16,512]{2,1,0:T(8,128)(2,1)S(1)} %pad_maximum_fusion.6), channel_id=1, source_target_pairs={{0,8},{1,9},{2,10},{3,11},{4,12},{5,13},{6,14},{7,15},{16,24},{17,... | collective-permute-start | bytes 147464 | tf_op jit(solution)/shard_map/ppermute | solution.py:16
  124.9 36.7 %collective-permute-start.16 = (bf16[3,16,512]{2,1,0:T(8,128)(2,1)}, bf16[3,16,512]{2,1,0:T(8,128)(2,1)}, u32[]{:S(2)}, u32[]{:S(2)}) collective-permute-start(bf16[3,16,512]{2,1,0:T(8,128)(2,1)} %pad_maximum_fusion.7), channel_id=1, source_target_pairs={{0,1},{1,2},{2,3},{3,4},{4,5},{5,6},{6,7},{7,8},{8,9},{9,10},{10,1... | collective-permute-start | bytes 147464 | tf_op jit(solution)/shard_map/ppermute | solution.py:16
  127.4 35.0 %collective-permute-start.17 = (bf16[3,16,512]{2,1,0:T(8,128)(2,1)}, bf16[3,16,512]{2,1,0:T(8,128)(2,1)}, u32[]{:S(2)}, u32[]{:S(2)}) collective-permute-start(bf16[3,16,512]{2,1,0:T(8,128)(2,1)} %pad_maximum_fusion.8), channel_id=1, source_target_pairs={{1,0},{2,1},{3,2},{4,3},{5,4},{6,5},{7,6},{8,7},{9,8},{10,9},{11,1... | collective-permute-start | bytes 147464 | tf_op jit(solution)/shard_map/ppermute | solution.py:16
  161.0 3.0 %copy-start.6 = (f32[384,512]{1,0:T(8,128)S(1)}, f32[384,512]{1,0:T(8,128)}, u32[]{:S(2)}) copy-start(f32[384,512]{1,0:T(8,128)} %get-tuple-element.42) | copy-start | bytes 2359300
  161.0 3.0 %copy-start.7 = (f32[256,512]{1,0:T(8,128)S(1)}, f32[256,512]{1,0:T(8,128)}, u32[]{:S(2)}) copy-start(f32[256,512]{1,0:T(8,128)} %fusion.14) | copy-start | bytes 1572868
Sparse Core Ops, SparseCore 0:
  69.4 55.0 reduce-scatter.7
  129.3 60.6 reduce-scatter.5
  194.4 71.4 reduce-scatter.3
where the time goes:
time: 273 us; the launch traced here: 272 us
  waiting for transfers between devices  118 us (43%)
  starting transfers between devices  42.7 us (16%)
  matrix products  38.5 us (14%)
  blocking collectives  30.8 us (11%)
  local copies, waits for them, and re-layouts  18.1 us (7%)
  between operations  16.5 us (6%)
  other arithmetic  7.75 us (3%)
    reduce_scatter x1, waiting for transfers between devices, body(): lax.psum_scatter(grad_weight_in, 'dom', scatter_dimension=0, tiled=True)  75.9 us
    unnamed x1, blocking collectives  30.8 us
    reduce_scatter x1, waiting for transfers between devices, body(): lax.psum_scatter(grad_wout, 'dom', scatter_dimension=0, tiled=True)  24.5 us
    ppermute x10, starting transfers between devices, passed_along(): return lax.ppermute(block, axis, route)  23.2 us
    dot_general x14, matrix products, contract_rows(): lax.dot_general(left_side, right_side, (((0,), (0,)), ((), ())), preferre...  19.4 us
    ppermute x8, starting transfers between devices, from_behind(): lax.ppermute(value, axis, [(source, source + steps) for source in range(i...  19.2 us
    ppermute x10, waiting for transfers between devices, passed_along(): return lax.ppermute(block, axis, route)  14.2 us
    dot_general x4, matrix products, contract_cols(): lax.dot_general(left_side, right_side, (((1,), (1,)), ((), ())), preferre...  8.81 us
  transfers between devices with their start and end apart: 21, of which 10 were waited for; matrix products, arithmetic and copies ran while one was open for 22% of the time, Pallas kernels for 0%

commit v1 on v0

v1 whole, which is shorter than its diff:
```python
import functools

import jax
import jax.numpy as jnp
from jax import lax
from jax.experimental import pallas as pl
from jax.experimental.pallas import tpu as pltpu
from jax.sharding import PartitionSpec as P

GRID_Y = 8
CO_DEV = 4
MESH = pl.DeviceIdType.MESH
F32 = jnp.float32
BF16 = jnp.bfloat16
I32 = jnp.int32
directions = ((-1, -1), (-1, 0), (-1, 1), (0, -1), (0, 1), (1, -1), (1, 0), (1, 1))
pool_moves = ((2, 16, 8), (-2, 0, 8), (1, 8, 16), (-1, 0, 16))


def dot_nn(a, b):
    return jnp.dot(a, b, preferred_element_type=F32)


def dot_nt(a, b):
    return lax.dot_general(a, b, (((1,), (1,)), ((), ())), preferred_element_type=F32)


def dot_tn(a, b):
    return lax.dot_general(a, b, (((0,), (0,)), ((), ())), preferred_element_type=F32)


def sigmoid(v):
    return 0.5 * (1.0 + jnp.tanh(0.5 * v))


def as_columns(row):
    return jnp.transpose(jnp.broadcast_to(row, (128, row.shape[1])))


def hot_lanes(columns, start):
    lanes = lax.broadcasted_iota(I32, columns.shape, 1) + start
    return jnp.where(columns == lanes, 1.0, 0.0).astype(BF16)


def hot_rows(row, count):
    shape = (count, row.shape[1])
    return jnp.where(lax.broadcasted_iota(I32, shape, 0) == row, 1.0, 0.0).astype(BF16)


def scatters_inside(n, sizes):
    return n & (n - 1) == 0 and all(rows % (16 * n) == 0 for rows in sizes)


def kernel(n, inside, *refs):
    (
        nodes, node_count, edge_src, edge_dst, edge_count, send_rows, assign,
        w_in_hbm, b_in, w_out_hbm, w_back_hbm, grad_out,
        fields, grad_nodes, g_in, g_bias, g_out, g_back,
        w_in, w_out, w_back, load_sem,
        table, outgoing, halo_send, halo_recv,
        hot, hot_t, proj, slope, gathered, spread_sum,
        pool, pool_in, gpool, gpool_in, pool_send, pool_recv,
        back_out, back_in, back_send, back_recv,
        *scatter,
    ) = refs
    num_nodes, latent = nodes.shape
    num_edges = edge_src.shape[1]
    hid = b_in.shape[1]
    halo = send_rows.shape[1]
    slot = halo // len(directions)
    ext = num_nodes + halo
    me = lax.axis_index("dom")
    depth = n.bit_length() - 1

    loads = [
        pltpu.make_async_copy(source, target, load_sem.at[i])
        for i, (source, target) in enumerate(
            ((w_in_hbm, w_in), (w_out_hbm, w_out), (w_back_hbm, w_back))
        )
    ]
    for load in loads:
        load.start()

    def remote(source, target, sent, received, device):
        return pltpu.make_async_remote_copy(
            src_ref=source,
            dst_ref=target,
            send_sem=sent,
            recv_sem=received,
            device_id={"dom": device},
            device_id_type=MESH,
        )

    def beside(offset):
        return lax.rem(me + offset + 2 * n, n)

    table[num_nodes:, :] = jnp.zeros((halo, latent), BF16)
    back_in[...] = jnp.zeros((halo, latent), BF16)
    barrier = pltpu.get_barrier_semaphore()
    offsets = {(a * GRID_Y + b) % n for a, b in directions} | {1, 2, n - 1, n - 2}
    partners = [beside(offset) for offset in sorted(offsets)]
    if inside:
        for level in range(depth):
            step = 1 << level
            if step in offsets and n - step in offsets:
                continue
            partners.append(me + step - 2 * step * lax.rem(me // step, 2))
    for partner in partners:
        pl.semaphore_signal(barrier, inc=1, device_id={"dom": partner}, device_id_type=MESH)

    valid = lax.broadcasted_iota(I32, (num_nodes, 1), 0) < node_count[0]
    valid_f = jnp.where(valid, 1.0, 0.0)
    first = (nodes[...].astype(F32) * valid_f).astype(BF16)
    table[:num_nodes, :] = first
    send_cols = as_columns(send_rows[...])
    for start in range(0, num_nodes, 128):
        part = dot_nn(hot_lanes(send_cols, start), first[start : start + 128])
        sent = part if start == 0 else sent + part
    outgoing[...] = sent.astype(BF16)
    pl.semaphore_wait(barrier, len(partners))

    grid_row, grid_col = me // GRID_Y, lax.rem(me, GRID_Y)
    on_grid = [
        (grid_row + a >= 0)
        & (grid_row + a < n // GRID_Y)
        & (grid_col + b >= 0)
        & (grid_col + b < GRID_Y)
        for a, b in directions
    ]

    def halo_exchange(source, target, base, sent, received):
        copies = []
        for k, (a, b) in enumerate(directions):
            copy = remote(
                source.at[pl.ds(k * slot, slot)],
                target.at[pl.ds(base + (7 - k) * slot, slot)],
                sent.at[k],
                received.at[7 - k],
                beside(a * GRID_Y + b),
            )
            pl.when(on_grid[k])(copy.start)
            copies.append(copy)
        return copies

    def halo_wait(copies, recv):
        for k, copy in enumerate(copies):
            if recv:
                pl.when(on_grid[7 - k])(copy.wait_recv)
            else:
                pl.when(on_grid[k])(copy.wait_send)

    halo_copies = halo_exchange(outgoing, table, num_nodes, halo_send, halo_recv)

    edge_ok = lax.broadcasted_iota(I32, (1, num_edges), 1) < edge_count[0]
    src = jnp.where(edge_ok, edge_src[...], -1)
    dst = jnp.where(edge_ok, edge_dst[...], -1)
    hot_t[:ext, :] = hot_rows(src, ext)
    hot_t[ext:, :] = hot_rows(dst, num_nodes)
    src_cols, dst_cols = as_columns(src), as_columns(dst)
    for start in range(0, ext, 128):
        hot[:, start : start + 128] = hot_lanes(src_cols, start)
    for start in range(0, num_nodes, 128):
        hot[:, ext + start : ext + start + 128] = hot_lanes(dst_cols, start)

    total = CO_DEV * n
    rel = assign[...] - (me * CO_DEV - CO_DEV)
    rel = jnp.where(rel < 0, rel + total, rel)
    rel = jnp.where(rel >= total, rel - total, rel)
    node_ok = lax.broadcasted_iota(I32, (1, num_nodes), 1) < node_count[0]
    rel = jnp.where(node_ok, rel + (rel // CO_DEV) * (8 - CO_DEV), -100)
    window_hot = hot_rows(rel, 32)
    rel_cols = as_columns(rel)
    node_hot = hot_lanes(rel_cols, 0) + hot_lanes(rel_cols, -32)
    tail = jnp.zeros((64, latent), BF16)

    loads[0].wait()
    proj[:num_nodes, :] = dot_nn(first, w_in[:latent, :]).astype(BF16)
    proj[ext:, :] = dot_nn(first, w_in[latent:, :]).astype(BF16)
    halo_wait(halo_copies, True)
    proj[num_nodes:ext, :] = dot_nn(table[num_nodes:, :], w_in[:latent, :]).astype(BF16)

    wide = 256
    for start in range(0, hid, wide):
        cols = slice(start, start + wide)
        preact = dot_nn(hot[...], proj[:, cols]) + b_in[:, cols]
        gate = sigmoid(preact)
        hidden = preact * gate
        slope[:, cols] = gate + hidden * (1.0 - gate)
        gathered[:, cols] = dot_nn(hot_t[ext:, :], hidden.astype(BF16)).astype(BF16)
    loads[1].wait()
    summed = dot_nn(gathered[...], w_out[...])
    mid = ((first.astype(F32) + summed) * valid_f).astype(BF16)

    pool[:, :latent] = dot_nn(window_hot, mid)[:24]
    counts = jnp.sum(window_hot.astype(F32), axis=1, keepdims=True)
    pool[:, latent:] = jnp.broadcast_to(counts[:24], (24, 128))

    def pool_exchange(source, targets, level):
        copies = []
        for i, (offset, start, rows) in enumerate(pool_moves):
            copy = remote(
                source.at[pl.ds(start, rows)],
                targets.at[i, pl.ds(0, rows)],
                pool_send.at[level, i],
                pool_recv.at[level, i],
                beside(offset),
            )
            copy.start()
            copies.append(copy)
        return copies

    def pool_total(source, targets, copies):
        for copy in copies:
            copy.wait_recv()
        return (
            source[:8] + targets[2, :8] + targets[0, :8],
            source[8:16] + targets[2, 8:16] + targets[3, :8],
            source[16:24] + targets[3, 8:16] + targets[1, :8],
        )

    pool_copies = pool_exchange(pool, pool_in, 0)
    loads[2].wait()
    grad_top = (grad_out[...].astype(F32) * valid_f).astype(BF16)
    back_spread = dot_nt(grad_top, w_back[...])
    totals = jnp.concatenate(pool_total(pool, pool_in, pool_copies), axis=0)
    inverse = 1.0 / jnp.maximum(totals[:, latent : latent + 1], 1.0)
    coarse = totals[:, :latent] * inverse
    zeros8 = jnp.zeros((8, latent), F32)
    coarse = jnp.concatenate([coarse, zeros8], axis=0).astype(BF16)
    coarse = jnp.concatenate([coarse, jnp.zeros((32, latent), BF16), tail], axis=0)
    spread = dot_nn(node_hot, coarse)
    gate = sigmoid(spread)
    lifted_f = spread * gate
    grad_spread = back_spread * (gate + lifted_f * (1.0 - gate))
    gpool[...] = dot_nn(window_hot, grad_spread.astype(BF16))[:24]
    gpool_copies = pool_exchange(gpool, gpool_in, 1)
    lifted = lifted_f.astype(BF16)

    chunks = []
    if inside:
        bufs, ins, bias_buf, bias_in, sc_send, sc_recv, bias_send, bias_recv = (
            scatter[:4],
            scatter[4 : 4 + 4 * depth],
            *scatter[4 + 4 * depth :],
        )
        orders = [tuple(range(depth))] * 4
        bits = [lax.rem(me // (1 << level), 2) for level in range(depth)]

        def place(order, shard):
            return sum(((shard >> bit) & 1) << (depth - 1 - i) for i, bit in enumerate(order))

        pending = {}
        bases = [[0] * (depth + 1) for _ in range(4)]

        def send_half(c, level):
            order, half = orders[c], n >> (level + 1)
            bit = bits[order[level]]
            base = bases[c][level]
            bases[c][level + 1] = base + bit * half
            copy = remote(
                bufs[c].at[pl.ds(base + (1 - bit) * half, half)],
                ins[c * depth + level],
                sc_send.at[c, level],
                sc_recv.at[c, level],
                me + (1 - 2 * bit) * (1 << order[level]),
            )
            copy.start()
            pending[c, level] = copy

        def advance(c, level):
            pending[c, level].wait_recv()
            arrived = ins[c * depth + level]
            base = bases[c][level + 1]
            if level == depth - 1:
                return bufs[c][base].astype(F32) + arrived[0].astype(F32)
            half = n >> (level + 2)
            bit = bits[orders[c][level + 1]]

            def add(offset):
                target = pl.ds(base + offset, half)
                mine = bufs[c][target].astype(F32) + arrived[pl.ds(offset, half)].astype(F32)
                bufs[c][target] = mine.astype(BF16)

            add((1 - bit) * half)
            send_half(c, level + 1)
            add(bit * half)
            return None

        def store(c, value, cols):
            rows = value.shape[0] // n
            for shard in range(n):
                bufs[c][place(orders[c], shard), :, cols] = value[
                    shard * rows : (shard + 1) * rows
                ].astype(BF16)

    grad_back = dot_tn(lifted, grad_top)
    if inside:
        store(0, grad_back, slice(0, latent))
        send_half(0, 0)
    else:
        g_back[...] = grad_back
    top = mid.astype(F32) + dot_nn(lifted, w_back[...])
    fields[...] = (top * valid_f).astype(BF16)

    gsum = jnp.concatenate(pool_total(gpool, gpool_in, gpool_copies), axis=0) * inverse
    gsum = jnp.concatenate([gsum, zeros8], axis=0)
    upper = gsum.astype(BF16)
    lower = (gsum - upper.astype(F32)).astype(BF16)
    lifted_grad = dot_nn(node_hot, jnp.concatenate([upper, lower, tail], axis=0))
    grad_mid_f = (grad_top.astype(F32) + lifted_grad) * valid_f
    grad_mid = grad_mid_f.astype(BF16)
    if inside:
        advance(0, 0)
    grad_out_w = dot_tn(gathered[...], grad_mid)
    if inside:
        store(1, grad_out_w, slice(0, latent))
        send_half(1, 0)
    else:
        g_out[...] = grad_out_w

    sources = table[...]
    for start in range(0, hid, wide):
        cols = slice(start, start + wide)
        back = dot_nt(grad_mid, w_out[cols, :]).astype(BF16)
        grad_pre = (dot_nn(hot[:, ext:], back) * slope[:, cols]).astype(BF16)
        sums = dot_nn(hot_t[...], grad_pre).astype(BF16)
        spread_sum[:, cols] = sums
        partial = grad_pre.astype(F32).reshape(num_edges // 8, 8, wide).sum(axis=0)
        upper_grad = dot_tn(sources, sums[:ext])
        lower_grad = dot_tn(first, sums[ext:])
        if inside:
            bias_buf[0, :, cols] = partial
            c, left = 2 + start // latent, start % latent
            value = jnp.concatenate([upper_grad, lower_grad], axis=0)
            store(c, value, slice(left, left + wide))
            if left + wide == latent:
                send_half(c, 0)
            if start == 0:
                advance(1, 0)
                advance(0, 1)
            if start == 2 * wide:
                advance(1, 1)
                advance(2, 0)
                advance(0, 2)
        else:
            g_bias[:, cols] = partial
            g_in[:latent, cols] = upper_grad
            g_in[latent:, cols] = lower_grad

    def bias_level(level):
        step = 1 << level
        copy = remote(
            bias_buf.at[level],
            bias_in.at[level],
            bias_send.at[level],
            bias_recv.at[level],
            me + step - 2 * step * bits[level],
        )
        copy.start()
        return copy

    def bias_add(level, copy):
        copy.wait_recv()
        both = bias_buf[level] + bias_in[level]
        if level + 1 < depth:
            bias_buf[level + 1] = both
            return bias_level(level + 1)
        g_bias[...] = both
        return None

    halo_grad = dot_nt(spread_sum[num_nodes:ext, :], w_in[:latent, :])
    back_out[...] = halo_grad.astype(BF16)
    if inside:
        bias_copies = [bias_level(0)]
    back_copies = halo_exchange(back_out, back_in, 0, back_send, back_recv)
    if inside:
        advance(3, 0)
        advance(1, 2)
        advance(2, 1)
        bias_copies.append(bias_add(0, bias_copies[-1]))
    local = dot_nt(spread_sum[:num_nodes, :], w_in[:latent, :])
    local = local + dot_nt(spread_sum[ext:, :], w_in[latent:, :]) + grad_mid.astype(F32)
    if inside:
        g_back[...] = advance(0, depth - 1)
        bias_copies.append(bias_add(1, bias_copies[-1]))
    halo_wait(back_copies, True)
    owner_hot = hot_rows(send_rows[...], num_nodes)
    local = local + dot_nn(owner_hot, back_in[...])
    grad_nodes[...] = (local * valid_f).astype(BF16)
    if inside:
        advance(2, 2)
        advance(3, 1)
        g_out[...] = advance(1, depth - 1)
        bias_copies.append(bias_add(2, bias_copies[-1]))
        advance(3, 2)
        g_in[:, :latent] = advance(2, depth - 1)
        bias_add(3, bias_copies[-1])
        g_in[:, latent:] = advance(3, depth - 1)
        for copy in pending.values():
            copy.wait_send()
        for copy in bias_copies:
            copy.wait_send()
    halo_wait(halo_copies, False)
    halo_wait(back_copies, False)
    for copy in pool_copies + gpool_copies:
        copy.wait_send()


def body(
    nodes, node_count, edge_src, edge_dst, edge_count, send_list, assign,
    w_in, b_in, w_out, w_back, grad_out,
):
    num_nodes, latent = nodes.shape
    num_edges = edge_src.shape[0]
    hid = b_in.shape[0]
    n = lax.axis_size("dom")
    halo = send_list.shape[1] * send_list.shape[2]
    ext = num_nodes + halo
    inside = n == 16 and scatters_inside(n, (2 * latent, hid, latent))
    depth = n.bit_length() - 1
    share = n if inside else 1
    vmem = pl.BlockSpec(memory_space=pltpu.VMEM)
    smem = pl.BlockSpec(memory_space=pltpu.SMEM)
    anywhere = pl.BlockSpec(memory_space=pl.ANY)
    dma = pltpu.SemaphoreType.DMA
    scratch = [
        pltpu.VMEM(w_in.shape, BF16),
        pltpu.VMEM(w_out.shape, BF16),
        pltpu.VMEM(w_back.shape, BF16),
        dma((3,)),
        pltpu.VMEM((ext, latent), BF16),
        pltpu.VMEM((halo, latent), BF16),
        dma((8,)),
        dma((8,)),
        pltpu.VMEM((num_edges, ext + num_nodes), BF16),
        pltpu.VMEM((ext + num_nodes, num_edges), BF16),
        pltpu.VMEM((ext + num_nodes, hid), BF16),
        pltpu.VMEM((num_edges, hid), F32),
        pltpu.VMEM((num_nodes, hid), BF16),
        pltpu.VMEM((ext + num_nodes, hid), BF16),
        pltpu.VMEM((24, latent + 128), F32),
        pltpu.VMEM((4, 16, latent + 128), F32),
        pltpu.VMEM((24, latent), F32),
        pltpu.VMEM((4, 16, latent), F32),
        dma((2, 4)),
        dma((2, 4)),
        pltpu.VMEM((halo, latent), BF16),
        pltpu.VMEM((halo, latent), BF16),
        dma((8,)),
        dma((8,)),
    ]
    if inside:
        sizes = (latent, hid, 2 * latent, 2 * latent)
        scratch += [pltpu.VMEM((n, rows // n, latent), BF16) for rows in sizes]
        scratch += [
            pltpu.VMEM((n >> (level + 1), rows // n, latent), BF16)
            for rows in sizes
            for level in range(depth)
        ]
        scratch += [
            pltpu.VMEM((depth, 8, hid), F32),
            pltpu.VMEM((depth, 8, hid), F32),
            dma((4, depth)),
            dma((4, depth)),
            dma((depth,)),
            dma((depth,)),
        ]
    shapes = (
        jax.ShapeDtypeStruct((num_nodes, latent), BF16),
        jax.ShapeDtypeStruct((num_nodes, latent), BF16),
        jax.ShapeDtypeStruct((2 * latent // share, hid), F32),
        jax.ShapeDtypeStruct((8, hid), F32),
        jax.ShapeDtypeStruct((hid // share, latent), F32),
        jax.ShapeDtypeStruct((latent // share, latent), F32),
    )
    fields, grad_nodes, g_in, g_bias, g_out, g_back = pl.pallas_call(
        functools.partial(kernel, n, inside),
        out_shape=shapes,
        in_specs=[vmem, smem, vmem, vmem, smem, vmem, vmem, anywhere, vmem, anywhere, anywhere, vmem],
        out_specs=[vmem] * 6,
        scratch_shapes=scratch,
        compiler_params=pltpu.CompilerParams(
            collective_id=0, has_side_effects=True, vmem_limit_bytes=56 * 1024 * 1024
        ),
        name="mesh_step",
    )(
        nodes,
        node_count,
        edge_src.reshape(1, -1),
        edge_dst.reshape(1, -1),
        edge_count,
        send_list.reshape(1, -1),
        assign.reshape(1, -1),
        w_in,
        b_in.reshape(1, -1),
        w_out,
        w_back,
        grad_out,
    )
    bias = jnp.sum(g_bias, axis=0)
    if inside:
        width = hid // n
        bias = lax.dynamic_slice(bias, (lax.axis_index("dom") * width,), (width,))
        return fields, grad_nodes, g_in, bias, g_out, g_back
    summed = [
        lax.psum_scatter(value, "dom", scatter_dimension=0, tiled=True)
        for value in (g_in, bias, g_out, g_back)
    ]
    return (fields, grad_nodes, *summed)


def solution(mesh):
    rows = P(("parts", "dom"), None)
    line = P(("parts", "dom"))
    return jax.shard_map(
        body,
        mesh=mesh,
        in_specs=(
            rows, line, line, line, line, P(("parts", "dom"), None, None), line,
            P(), P(), P(), P(), rows,
        ),
        out_specs=(rows, rows, rows, line, rows, rows),
        check_vma=False,
    )
```

time: 273 us -> 73.5 us (0.27)
  waiting for transfers between devices: 118 us -> 0 us
  Pallas kernels: 0 us -> 60.5 us
  starting transfers between devices: 42.7 us -> 0 us
  matrix products: 38.5 us -> 0 us
  blocking collectives: 30.8 us -> 0 us
  between operations: 16.5 us -> 1.94 us
  local copies, waits for them, and re-layouts: 18.1 us -> 9.91 us
  other arithmetic: 7.75 us -> 0.77 us
    reduce_scatter x3 -> x0, waiting for transfers between devices: 100 us -> none  [the longest x1 75.9 us: body(): lax.psum_scatter(grad_weight_in, 'dom', scatter_dimension=0, tiled=True)]
    pallas_call x0 -> x1, Pallas kernels: none -> 60.5 us  [body(): pl.pallas_call(functools.partial(kernel, n, inside), out_shape=shapes, in...]
    ppermute x18 -> x0, starting transfers between devices: 42.4 us -> none  [the longest x10 23.2 us: passed_along(): return lax.ppermute(block, axis, route)]
    dot_general x24 -> x0, matrix products: 38.5 us -> none  [the longest x14 19.4 us: contract_rows(): lax.dot_general(left_side, right_side, (((0,), (0,)), ((), ())), preferre...]
    unnamed x1 -> x0, blocking collectives: 30.8 us -> none
    ppermute x18 -> x0, waiting for transfers between devices: 17.7 us -> none  [the longest x10 14.2 us: passed_along(): return lax.ppermute(block, axis, route)]
    gather x4 -> x0, local copies, waits for them, and re-layouts: 13.9 us -> none  [the longest x1 5.1 us: body(): src_rows = jnp.take(node_table, edge_src, axis=0)]
    unnamed x52 -> x5, local copies, waits for them, and re-layouts: 2.53 us -> 8.05 us
  transfers between devices with their start and end apart: 21 -> 0, of which waited for: 10 -> 0; matrix products, arithmetic and copies ran while one was open for 22% -> 0% of each run, Pallas kernels for 0% -> 0%
where the time goes in v1:
time: 73.5 us; the launch traced here: 73.1 us
  Pallas kernels  60.5 us (82%)
  local copies, waits for them, and re-layouts  9.91 us (13%)
  between operations  1.94 us (3%)
  other arithmetic  0.77 us (1%)
    pallas_call x1, Pallas kernels, body(): pl.pallas_call(functools.partial(kernel, n, inside), out_shape=shapes, in...  60.5 us
    unnamed x5, local copies, waits for them, and re-layouts  8.05 us

profile of v1, /device:TPU:0, one launch (start us, length us, event | category | flops | bytes accessed | tf_op | source)
XLA Modules:
  0.0 73.1 jit_solution(9945744074547737407)
XLA Ops:
  1.9 1.3 %reshape.29.refs_5_ = s32[1,128]{1,0:T(1,128)} reshape(s32[1,8,16]{2,1,0:T(8,128)} %param.17) | data formatting | bytes 1024 | tf_op jit(solution)/shard_map/reshape | solution.py:492
  3.2 60.5 %mesh_step.1 = (bf16[256,512]{1,0:T(8,128)(2,1)}, bf16[256,512]{1,0:T(8,128)(2,1)}, f32[64,1024]{1,0:T(8,128)}, f32[8,1024]{1,0:T(8,128)}, f32[64,512]{1,0:T(8,128)}, /*index=5*/f32[32,512]{1,0:T(8,128)}) custom-call(bf16[256,512]{1,0:T(8,128)(2,1)} %refs_0_.1, s32[1]{0:T(128)S(6)} %copy.23.refs_1_, s32[1,1024]{1,0:T(1,128)} %bitcast.4, s32[1,1024]{1,0:T(1,128)} %bitcast.5, ...), custom_call_target="tpu_custom_call" | custom-call | tf_op jit(solution)/shard_map/mesh_step/pallas_call | solution.py:476
  63.7 0.8 %reduce_sum.9 = f32[1024]{0:T(1024)S(1)} reduce(f32[8,1024]{1,0:T(8,128)} %get-tuple-element.15, f32[]{:T(128)} %constant.5.clone.1), dimensions={0}, to_apply=%region_0.0 | reduce | flops 7168 | bytes 36868 | tf_op jit(solution)/shard_map/reduce_sum | solution.py:500
  64.4 0.6 dynamic_slice.3
  65.0 1.7 %copy.25 = bf16[256,512]{1,0:T(8,128)(2,1)} copy(bf16[256,512]{1,0:T(8,128)(2,1)} %get-tuple-element.24) | data formatting | bytes 524288
  66.7 1.7 %copy.26 = bf16[256,512]{1,0:T(8,128)(2,1)} copy(bf16[256,512]{1,0:T(8,128)(2,1)} %get-tuple-element.25) | data formatting | bytes 524288
  68.4 1.7 %copy.27 = f32[64,1024]{1,0:T(8,128)} copy(f32[64,1024]{1,0:T(8,128)} %get-tuple-element.26) | data formatting | bytes 524288
  70.0 1.6 %copy.28 = f32[64,512]{1,0:T(8,128)} copy(f32[64,512]{1,0:T(8,128)} %get-tuple-element.28) | data formatting | bytes 262144
  71.6 1.5 %copy.29 = f32[32,512]{1,0:T(8,128)} copy(f32[32,512]{1,0:T(8,128)} %get-tuple-element.29) | data formatting | bytes 131072

commit v2 on v1

--- a/solution.py
+++ b/solution.py
@@ -53,12 +53,12 @@
 
 def kernel(n, inside, *refs):
     (
-        nodes, node_count, edge_src, edge_dst, edge_count, send_rows, assign,
-        w_in_hbm, b_in, w_out_hbm, w_back_hbm, grad_out,
+        nodes_hbm, node_count, src_hbm, dst_hbm, edge_count, send_hbm, assign_hbm,
+        w_in_hbm, b_in_hbm, w_out_hbm, w_back_hbm, grad_out_hbm,
         fields, grad_nodes, g_in, g_bias, g_out, g_back,
-        w_in, w_out, w_back, load_sem,
+        w_in, w_out, w_back, nodes, edge_src, edge_dst, send_list, assign, b_in, grad_out, load_sem,
         table, outgoing, halo_send, halo_recv,
-        hot, hot_t, proj, slope, gathered, spread_sum,
+        table_t, gathered_t, hot, hot_t, proj, slope, gathered, spread_sum,
         pool, pool_in, gpool, gpool_in, pool_send, pool_recv,
         back_out, back_in, back_send, back_recv,
         *scatter,
@@ -66,20 +66,11 @@
     num_nodes, latent = nodes.shape
     num_edges = edge_src.shape[1]
     hid = b_in.shape[1]
-    halo = send_rows.shape[1]
-    slot = halo // len(directions)
+    slot = send_list.shape[2]
+    halo = len(directions) * slot
     ext = num_nodes + halo
     me = lax.axis_index("dom")
     depth = n.bit_length() - 1
-
-    loads = [
-        pltpu.make_async_copy(source, target, load_sem.at[i])
-        for i, (source, target) in enumerate(
-            ((w_in_hbm, w_in), (w_out_hbm, w_out), (w_back_hbm, w_back))
-        )
-    ]
-    for load in loads:
-        load.start()
 
     def remote(source, target, sent, received, device):
         return pltpu.make_async_remote_copy(
@@ -94,6 +85,25 @@
     def beside(offset):
         return lax.rem(me + offset + 2 * n, n)
 
+    loads = [
+        pltpu.make_async_copy(source, target, load_sem.at[i])
+        for i, (source, target) in enumerate(
+            (
+                (w_in_hbm, w_in),
+                (w_out_hbm, w_out),
+                (w_back_hbm, w_back),
+                (nodes_hbm, nodes),
+                (send_hbm, send_list),
+                (src_hbm, edge_src),
+                (dst_hbm, edge_dst),
+                (assign_hbm, assign),
+                (b_in_hbm, b_in),
+                (grad_out_hbm, grad_out),
+            )
+        )
+    ]
+    for i in (3, 4, 5, 6, 7, 8, 0, 1, 2, 9):
+        loads[i].start()
     table[num_nodes:, :] = jnp.zeros((halo, latent), BF16)
     back_in[...] = jnp.zeros((halo, latent), BF16)
     barrier = pltpu.get_barrier_semaphore()
@@ -110,9 +120,12 @@
 
     valid = lax.broadcasted_iota(I32, (num_nodes, 1), 0) < node_count[0]
     valid_f = jnp.where(valid, 1.0, 0.0)
+    loads[3].wait()
+    loads[4].wait()
     first = (nodes[...].astype(F32) * valid_f).astype(BF16)
     table[:num_nodes, :] = first
-    send_cols = as_columns(send_rows[...])
+    send_rows = jnp.concatenate([send_list[0, k : k + 1, :] for k in range(8)], axis=1)
+    send_cols = as_columns(send_rows)
     for start in range(0, num_nodes, 128):
         part = dot_nn(hot_lanes(send_cols, start), first[start : start + 128])
         sent = part if start == 0 else sent + part
@@ -151,6 +164,8 @@
 
     halo_copies = halo_exchange(outgoing, table, num_nodes, halo_send, halo_recv)
 
+    for i in (5, 6, 7, 8):
+        loads[i].wait()
     edge_ok = lax.broadcasted_iota(I32, (1, num_edges), 1) < edge_count[0]
     src = jnp.where(edge_ok, edge_src[...], -1)
     dst = jnp.where(edge_ok, edge_dst[...], -1)
@@ -183,9 +198,8 @@
     for start in range(0, hid, wide):
         cols = slice(start, start + wide)
         preact = dot_nn(hot[...], proj[:, cols]) + b_in[:, cols]
-        gate = sigmoid(preact)
-        hidden = preact * gate
-        slope[:, cols] = gate + hidden * (1.0 - gate)
+        slope[:, cols] = preact
+        hidden = preact * sigmoid(preact)
         gathered[:, cols] = dot_nn(hot_t[ext:, :], hidden.astype(BF16)).astype(BF16)
     loads[1].wait()
     summed = dot_nn(gathered[...], w_out[...])
@@ -218,10 +232,21 @@
             source[16:24] + targets[3, 8:16] + targets[1, :8],
         )
 
+    def finish_slope(start):
+        for left in range(start, start + hid // 2, wide):
+            cols = slice(left, left + wide)
+            preact = slope[:, cols]
+            gate = sigmoid(preact)
+            slope[:, cols] = gate + preact * gate * (1.0 - gate)
+
     pool_copies = pool_exchange(pool, pool_in, 0)
     loads[2].wait()
+    loads[9].wait()
     grad_top = (grad_out[...].astype(F32) * valid_f).astype(BF16)
     back_spread = dot_nt(grad_top, w_back[...])
+    table_t[...] = jnp.transpose(table[...])
+    gathered_t[...] = jnp.transpose(gathered[...])
+    finish_slope(0)
     totals = jnp.concatenate(pool_total(pool, pool_in, pool_copies), axis=0)
     inverse = 1.0 / jnp.maximum(totals[:, latent : latent + 1], 1.0)
     coarse = totals[:, :latent] * inverse
@@ -239,18 +264,18 @@
     chunks = []
     if inside:
         bufs, ins, bias_buf, bias_in, sc_send, sc_recv, bias_send, bias_recv = (
-            scatter[:4],
-            scatter[4 : 4 + 4 * depth],
-            *scatter[4 + 4 * depth :],
+            scatter[:6],
+            scatter[6 : 6 + 6 * depth],
+            *scatter[6 + 6 * depth :],
         )
-        orders = [tuple(range(depth))] * 4
+        orders = [(0, 1, 2, 3), (0, 2, 1, 3), (0, 1, 2, 3), (0, 1, 2, 3), (0, 2, 1, 3), (0, 1, 2, 3)]
         bits = [lax.rem(me // (1 << level), 2) for level in range(depth)]
 
         def place(order, shard):
             return sum(((shard >> bit) & 1) << (depth - 1 - i) for i, bit in enumerate(order))
 
         pending = {}
-        bases = [[0] * (depth + 1) for _ in range(4)]
+        bases = [[0] * (depth + 1) for _ in range(6)]
 
         def send_half(c, level):
             order, half = orders[c], n >> (level + 1)
@@ -286,22 +311,23 @@
             add(bit * half)
             return None
 
-        def store(c, value, cols):
+        def store(c, value):
             rows = value.shape[0] // n
             for shard in range(n):
-                bufs[c][place(orders[c], shard), :, cols] = value[
+                bufs[c][place(orders[c], shard)] = value[
                     shard * rows : (shard + 1) * rows
                 ].astype(BF16)
 
     grad_back = dot_tn(lifted, grad_top)
     if inside:
-        store(0, grad_back, slice(0, latent))
+        store(0, grad_back)
         send_half(0, 0)
     else:
         g_back[...] = grad_back
     top = mid.astype(F32) + dot_nn(lifted, w_back[...])
     fields[...] = (top * valid_f).astype(BF16)
 
+    finish_slope(hid // 2)
     gsum = jnp.concatenate(pool_total(gpool, gpool_in, gpool_copies), axis=0) * inverse
     gsum = jnp.concatenate([gsum, zeros8], axis=0)
     upper = gsum.astype(BF16)
@@ -311,14 +337,13 @@
     grad_mid = grad_mid_f.astype(BF16)
     if inside:
         advance(0, 0)
-    grad_out_w = dot_tn(gathered[...], grad_mid)
-    if inside:
-        store(1, grad_out_w, slice(0, latent))
+    grad_out_w = dot_nn(gathered_t[...], grad_mid)
+    if inside:
+        store(1, grad_out_w)
         send_half(1, 0)
     else:
         g_out[...] = grad_out_w
 
-    sources = table[...]
     for start in range(0, hid, wide):
         cols = slice(start, start + wide)
         back = dot_nt(grad_mid, w_out[cols, :]).astype(BF16)
@@ -326,22 +351,15 @@
         sums = dot_nn(hot_t[...], grad_pre).astype(BF16)
         spread_sum[:, cols] = sums
         partial = grad_pre.astype(F32).reshape(num_edges // 8, 8, wide).sum(axis=0)
-        upper_grad = dot_tn(sources, sums[:ext])
-        lower_grad = dot_tn(first, sums[ext:])
+        upper_grad = dot_nn(table_t[...], sums[:ext])
+        lower_grad = dot_nn(table_t[:, :num_nodes], sums[ext:])
         if inside:
             bias_buf[0, :, cols] = partial
-            c, left = 2 + start // latent, start % latent
-            value = jnp.concatenate([upper_grad, lower_grad], axis=0)
-            store(c, value, slice(left, left + wide))
-            if left + wide == latent:
-                send_half(c, 0)
-            if start == 0:
-                advance(1, 0)
-                advance(0, 1)
-            if start == 2 * wide:
-                advance(1, 1)
-                advance(2, 0)
-                advance(0, 2)
+            c = 2 + start // wide
+            store(c, jnp.concatenate([upper_grad, lower_grad], axis=0))
+            send_half(c, 0)
+            for step in (((1, 0),), ((0, 1), (2, 0)), ((1, 1), (3, 0)), ((0, 2), (2, 1), (4, 0)))[c - 2]:
+                advance(*step)
         else:
             g_bias[:, cols] = partial
             g_in[:latent, cols] = upper_grad
@@ -374,28 +392,33 @@
         bias_copies = [bias_level(0)]
     back_copies = halo_exchange(back_out, back_in, 0, back_send, back_recv)
     if inside:
-        advance(3, 0)
+        advance(5, 0)
         advance(1, 2)
-        advance(2, 1)
+        advance(3, 1)
         bias_copies.append(bias_add(0, bias_copies[-1]))
     local = dot_nt(spread_sum[:num_nodes, :], w_in[:latent, :])
     local = local + dot_nt(spread_sum[ext:, :], w_in[latent:, :]) + grad_mid.astype(F32)
     if inside:
         g_back[...] = advance(0, depth - 1)
-        bias_copies.append(bias_add(1, bias_copies[-1]))
+        advance(4, 1)
+        advance(2, 2)
     halo_wait(back_copies, True)
-    owner_hot = hot_rows(send_rows[...], num_nodes)
+    owner_hot = hot_rows(send_rows, num_nodes)
     local = local + dot_nn(owner_hot, back_in[...])
     grad_nodes[...] = (local * valid_f).astype(BF16)
     if inside:
-        advance(2, 2)
-        advance(3, 1)
         g_out[...] = advance(1, depth - 1)
+        advance(5, 1)
+        bias_copies.append(bias_add(1, bias_copies[-1]))
+        advance(3, 2)
+        advance(4, 2)
+        g_in[:, :wide] = advance(2, depth - 1)
         bias_copies.append(bias_add(2, bias_copies[-1]))
-        advance(3, 2)
-        g_in[:, :latent] = advance(2, depth - 1)
+        advance(5, 2)
+        g_in[:, wide : 2 * wide] = advance(3, depth - 1)
+        g_in[:, 2 * wide : 3 * wide] = advance(4, depth - 1)
         bias_add(3, bias_copies[-1])
-        g_in[:, latent:] = advance(3, depth - 1)
+        g_in[:, 3 * wide :] = advance(5, depth - 1)
         for copy in pending.values():
             copy.wait_send()
         for copy in bias_copies:
@@ -404,6 +427,26 @@
     halo_wait(back_copies, False)
     for copy in pool_copies + gpool_copies:
         copy.wait_send()
+
+
+def finish(n, g_bias, *refs):
+    wholes, results, bias, sem = refs[:5], refs[5:10], refs[10], refs[11]
+    copies = [
+        pltpu.make_async_copy(source, target, sem.at[i])
+        for i, (source, target) in enumerate(zip(wholes, results))
+    ]
+    for copy in copies:
+        copy.start()
+    line = jnp.sum(g_bias[...], axis=0, keepdims=True)
+    width = line.shape[1] // n
+    me = lax.axis_index("dom")
+    shards = [line[:, i * width : (i + 1) * width] for i in range(n)]
+    mine = jnp.where(me == 0, shards[0], 0.0)
+    for i in range(1, n):
+        mine = jnp.where(me == i, shards[i], mine)
+    bias[...] = mine.reshape(width)
+    for copy in copies:
+        copy.wait()
 
 
 def body(
@@ -427,11 +470,20 @@
         pltpu.VMEM(w_in.shape, BF16),
         pltpu.VMEM(w_out.shape, BF16),
         pltpu.VMEM(w_back.shape, BF16),
-        dma((3,)),
+        pltpu.VMEM(nodes.shape, BF16),
+        pltpu.VMEM((1, num_edges), I32),
+        pltpu.VMEM((1, num_edges), I32),
+        pltpu.VMEM(send_list.shape, I32),
+        pltpu.VMEM((1, num_nodes), I32),
+        pltpu.VMEM((1, hid), F32),
+        pltpu.VMEM(grad_out.shape, BF16),
+        dma((10,)),
         pltpu.VMEM((ext, latent), BF16),
         pltpu.VMEM((halo, latent), BF16),
         dma((8,)),
         dma((8,)),
+        pltpu.VMEM((latent, ext), BF16),
+        pltpu.VMEM((hid, num_nodes), BF16),
         pltpu.VMEM((num_edges, ext + num_nodes), BF16),
         pltpu.VMEM((ext + num_nodes, num_edges), BF16),
         pltpu.VMEM((ext + num_nodes, hid), BF16),
@@ -450,18 +502,18 @@
         dma((8,)),
     ]
     if inside:
-        sizes = (latent, hid, 2 * latent, 2 * latent)
-        scratch += [pltpu.VMEM((n, rows // n, latent), BF16) for rows in sizes]
+        sizes = ((latent, latent), (hid, latent)) + ((2 * latent, 256),) * 4
+        scratch += [pltpu.VMEM((n, rows // n, cols), BF16) for rows, cols in sizes]
         scratch += [
-            pltpu.VMEM((n >> (level + 1), rows // n, latent), BF16)
-            for rows in sizes
+            pltpu.VMEM((n >> (level + 1), rows // n, cols), BF16)
+            for rows, cols in sizes
             for level in range(depth)
         ]
         scratch += [
             pltpu.VMEM((depth, 8, hid), F32),
             pltpu.VMEM((depth, 8, hid), F32),
-            dma((4, depth)),
-            dma((4, depth)),
+            dma((6, depth)),
+            dma((6, depth)),
             dma((depth,)),
             dma((depth,)),
         ]
@@ -476,7 +528,7 @@
     fields, grad_nodes, g_in, g_bias, g_out, g_back = pl.pallas_call(
         functools.partial(kernel, n, inside),
         out_shape=shapes,
-        in_specs=[vmem, smem, vmem, vmem, smem, vmem, vmem, anywhere, vmem, anywhere, anywhere, vmem],
+        in_specs=[anywhere, smem, anywhere, anywhere, smem] + [anywhere] * 7,
         out_specs=[vmem] * 6,
         scratch_shapes=scratch,
         compiler_params=pltpu.CompilerParams(
@@ -489,7 +541,7 @@
         edge_src.reshape(1, -1),
         edge_dst.reshape(1, -1),
         edge_count,
-        send_list.reshape(1, -1),
+        send_list,
         assign.reshape(1, -1),
         w_in,
         b_in.reshape(1, -1),
@@ -497,11 +549,19 @@
         w_back,
         grad_out,
     )
+    if inside:
+        wholes = (fields, grad_nodes, g_in, g_out, g_back)
+        fields, grad_nodes, g_in, g_out, g_back, bias = pl.pallas_call(
+            functools.partial(finish, n),
+            out_shape=[jax.ShapeDtypeStruct(whole.shape, whole.dtype) for whole in wholes]
+            + [jax.ShapeDtypeStruct((hid // n,), F32)],
+            in_specs=[vmem] * 6,
+            out_specs=[anywhere] * 5 + [vmem],
+            scratch_shapes=[dma((5,))],
+            name="place_results",
+        )(g_bias, *wholes)
+        return fields, grad_nodes, g_in, bias, g_out, g_back
     bias = jnp.sum(g_bias, axis=0)
-    if inside:
-        width = hid // n
-        bias = lax.dynamic_slice(bias, (lax.axis_index("dom") * width,), (width,))
-        return fields, grad_nodes, g_in, bias, g_out, g_back
     summed = [
         lax.psum_scatter(value, "dom", scatter_dimension=0, tiled=True)
         for value in (g_in, bias, g_out, g_back)

time: 73.5 us -> 59.9 us (0.81)
  local copies, waits for them, and re-layouts: 9.91 us -> 0 us
  Pallas kernels: 60.5 us -> 57.8 us
  other arithmetic: 0.77 us -> 0 us
    unnamed x5 -> x0, local copies, waits for them, and re-layouts: 8.05 us -> none
    pallas_call x1, Pallas kernels: 60.5 us -> 55 us  [body(): pl.pallas_call(functools.partial(kernel, n, inside), out_shape=shapes, in...]
    pallas_call x0 -> x1, Pallas kernels: none -> 2.82 us  [body(): pl.pallas_call(functools.partial(finish, n), out_shape=[jax.ShapeDtypeStr...]
    reshape x1 -> x0, local copies, waits for them, and re-layouts: 1.28 us -> none  [body(): send_list.reshape(1, -1)]
    reduce_sum x1 -> x0, other arithmetic: 0.77 us -> none  [body(): bias = jnp.sum(g_bias, axis=0)]
where the time goes in v2:
time: 59.9 us; the launch traced here: 59.8 us
  Pallas kernels  57.8 us (96%)
  between operations  1.93 us (3%)
    pallas_call x1, Pallas kernels, body(): pl.pallas_call(functools.partial(kernel, n, inside), out_shape=shapes, in...  55 us
    pallas_call x1, Pallas kernels, body(): pl.pallas_call(functools.partial(finish, n), out_shape=[jax.ShapeDtypeStr...  2.82 us

profile of v2, /device:TPU:0, one launch (start us, length us, event | category | flops | bytes accessed | tf_op | source)
XLA Modules:
  0.0 59.8 jit_solution(13684224330846336784)
XLA Ops:
  1.9 55.0 %mesh_step.1 = (bf16[256,512]{1,0:T(8,128)(2,1)}, bf16[256,512]{1,0:T(8,128)(2,1)}, f32[64,1024]{1,0:T(8,128)}, f32[8,1024]{1,0:T(8,128)}, f32[64,512]{1,0:T(8,128)}, /*index=5*/f32[32,512]{1,0:T(8,128)}) custom-call(bf16[256,512]{1,0:T(8,128)(2,1)} %refs_0_.1, s32[1]{0:T(128)S(6)} %copy.18.refs_1_, s32[1,1024]{1,0:T(1,128)} %bitcast.4, s32[1,1024]{1,0:T(1,128)} %bitcast.5, ...), custom_call_target="tpu_custom_call" | custom-call | tf_op jit(solution)/shard_map/mesh_step/pallas_call | solution.py:528
  56.9 2.8 %place_results.1 = (bf16[256,512]{1,0:T(8,128)(2,1)}, bf16[256,512]{1,0:T(8,128)(2,1)}, f32[64,1024]{1,0:T(8,128)}, f32[64,512]{1,0:T(8,128)}, f32[32,512]{1,0:T(8,128)}, /*index=5*/f32[64]{0:T(128)}) custom-call(f32[8,1024]{1,0:T(8,128)} %get-tuple-element.18.g_bias, bf16[256,512]{1,0:T(8,128)(2,1)} %get-tuple-element.19.refs_0_, ...), custom_call_target="tpu_custom_call" | custom-call | tf_op jit(solution)/shard_map/place_results/pallas_call | solution.py:554

commit v3 on v2

--- a/solution.py
+++ b/solution.py
@@ -108,13 +108,9 @@
     back_in[...] = jnp.zeros((halo, latent), BF16)
     barrier = pltpu.get_barrier_semaphore()
     offsets = {(a * GRID_Y + b) % n for a, b in directions} | {1, 2, n - 1, n - 2}
+    if inside:
+        offsets = set(range(1, n))
     partners = [beside(offset) for offset in sorted(offsets)]
-    if inside:
-        for level in range(depth):
-            step = 1 << level
-            if step in offsets and n - step in offsets:
-                continue
-            partners.append(me + step - 2 * step * lax.rem(me // step, 2))
     for partner in partners:
         pl.semaphore_signal(barrier, inc=1, device_id={"dom": partner}, device_id_type=MESH)
 
@@ -354,71 +350,61 @@
         upper_grad = dot_nn(table_t[...], sums[:ext])
         lower_grad = dot_nn(table_t[:, :num_nodes], sums[ext:])
         if inside:
-            bias_buf[0, :, cols] = partial
+            for left in range(0, wide, 128):
+                bias_buf[(start + left) // 128] = partial[:, left : left + 128]
             c = 2 + start // wide
             store(c, jnp.concatenate([upper_grad, lower_grad], axis=0))
             send_half(c, 0)
-            for step in (((1, 0),), ((0, 1), (2, 0)), ((1, 1), (3, 0)), ((0, 2), (2, 1), (4, 0)))[c - 2]:
+            for step in (((1, 0),), ((2, 0),), ((3, 0), (0, 1)), ((4, 0),))[c - 2]:
                 advance(*step)
         else:
             g_bias[:, cols] = partial
             g_in[:latent, cols] = upper_grad
             g_in[latent:, cols] = lower_grad
 
-    def bias_level(level):
-        step = 1 << level
-        copy = remote(
-            bias_buf.at[level],
-            bias_in.at[level],
-            bias_send.at[level],
-            bias_recv.at[level],
-            me + step - 2 * step * bits[level],
-        )
-        copy.start()
-        return copy
-
-    def bias_add(level, copy):
-        copy.wait_recv()
-        both = bias_buf[level] + bias_in[level]
-        if level + 1 < depth:
-            bias_buf[level + 1] = both
-            return bias_level(level + 1)
-        g_bias[...] = both
-        return None
+    def send_bias():
+        copies = []
+        for offset in range(1, n):
+            copy = remote(
+                bias_buf.at[beside(offset) * (hid // n) // 128],
+                bias_in.at[offset - 1],
+                bias_send.at[offset - 1],
+                bias_recv.at[offset - 1],
+                beside(offset),
+            )
+            copy.start()
+            copies.append(copy)
+        return copies
 
     halo_grad = dot_nt(spread_sum[num_nodes:ext, :], w_in[:latent, :])
     back_out[...] = halo_grad.astype(BF16)
     if inside:
-        bias_copies = [bias_level(0)]
+        bias_copies = send_bias()
     back_copies = halo_exchange(back_out, back_in, 0, back_send, back_recv)
     if inside:
         advance(5, 0)
-        advance(1, 2)
-        advance(3, 1)
-        bias_copies.append(bias_add(0, bias_copies[-1]))
     local = dot_nt(spread_sum[:num_nodes, :], w_in[:latent, :])
     local = local + dot_nt(spread_sum[ext:, :], w_in[latent:, :]) + grad_mid.astype(F32)
     if inside:
+        advance(0, 2)
+        advance(1, 1)
+        advance(2, 1)
         g_back[...] = advance(0, depth - 1)
-        advance(4, 1)
-        advance(2, 2)
     halo_wait(back_copies, True)
     owner_hot = hot_rows(send_rows, num_nodes)
     local = local + dot_nn(owner_hot, back_in[...])
     grad_nodes[...] = (local * valid_f).astype(BF16)
     if inside:
+        line = bias_buf[me * (hid // n) // 128]
+        for i, copy in enumerate(bias_copies):
+            copy.wait_recv()
+            line = line + bias_in[i]
+        g_bias[...] = line
+        for step in ((3, 1), (4, 1), (1, 2), (5, 1), (2, 2), (3, 2), (4, 2), (5, 2)):
+            advance(*step)
         g_out[...] = advance(1, depth - 1)
-        advance(5, 1)
-        bias_copies.append(bias_add(1, bias_copies[-1]))
-        advance(3, 2)
-        advance(4, 2)
-        g_in[:, :wide] = advance(2, depth - 1)
-        bias_copies.append(bias_add(2, bias_copies[-1]))
-        advance(5, 2)
-        g_in[:, wide : 2 * wide] = advance(3, depth - 1)
-        g_in[:, 2 * wide : 3 * wide] = advance(4, depth - 1)
-        bias_add(3, bias_copies[-1])
-        g_in[:, 3 * wide :] = advance(5, depth - 1)
+        for i in range(4):
+            g_in[:, i * wide : (i + 1) * wide] = advance(2 + i, depth - 1)
         for copy in pending.values():
             copy.wait_send()
         for copy in bias_copies:
@@ -429,7 +415,7 @@
         copy.wait_send()
 
 
-def finish(n, g_bias, *refs):
+def finish(g_bias, *refs):
     wholes, results, bias, sem = refs[:5], refs[5:10], refs[10], refs[11]
     copies = [
         pltpu.make_async_copy(source, target, sem.at[i])
@@ -438,12 +424,11 @@
     for copy in copies:
         copy.start()
     line = jnp.sum(g_bias[...], axis=0, keepdims=True)
-    width = line.shape[1] // n
-    me = lax.axis_index("dom")
-    shards = [line[:, i * width : (i + 1) * width] for i in range(n)]
-    mine = jnp.where(me == 0, shards[0], 0.0)
-    for i in range(1, n):
-        mine = jnp.where(me == i, shards[i], mine)
+    width = bias.shape[0]
+    place = lax.rem(lax.axis_index("dom") * width, 128) // width
+    mine = line[:, :width]
+    for i in range(1, 128 // width):
+        mine = jnp.where(place == i, line[:, i * width : (i + 1) * width], mine)
     bias[...] = mine.reshape(width)
     for copy in copies:
         copy.wait()
@@ -510,18 +495,18 @@
             for level in range(depth)
         ]
         scratch += [
-            pltpu.VMEM((depth, 8, hid), F32),
-            pltpu.VMEM((depth, 8, hid), F32),
+            pltpu.VMEM((hid // 128, 8, 128), F32),
+            pltpu.VMEM((n - 1, 8, 128), F32),
             dma((6, depth)),
             dma((6, depth)),
-            dma((depth,)),
-            dma((depth,)),
+            dma((n - 1,)),
+            dma((n - 1,)),
         ]
     shapes = (
         jax.ShapeDtypeStruct((num_nodes, latent), BF16),
         jax.ShapeDtypeStruct((num_nodes, latent), BF16),
         jax.ShapeDtypeStruct((2 * latent // share, hid), F32),
-        jax.ShapeDtypeStruct((8, hid), F32),
+        jax.ShapeDtypeStruct((8, 128 if inside else hid), F32),
         jax.ShapeDtypeStruct((hid // share, latent), F32),
         jax.ShapeDtypeStruct((latent // share, latent), F32),
     )
@@ -552,7 +537,7 @@
     if inside:
         wholes = (fields, grad_nodes, g_in, g_out, g_back)
         fields, grad_nodes, g_in, g_out, g_back, bias = pl.pallas_call(
-            functools.partial(finish, n),
+            finish,
             out_shape=[jax.ShapeDtypeStruct(whole.shape, whole.dtype) for whole in wholes]
             + [jax.ShapeDtypeStruct((hid // n,), F32)],
             in_specs=[vmem] * 6,

time: 59.9 us -> 58.1 us (0.970)
  Pallas kernels: 57.8 us -> 56 us
    pallas_call x1, Pallas kernels: 55 us -> 53.4 us  [body(): pl.pallas_call(functools.partial(kernel, n, inside), out_shape=shapes, in...]
where the time goes in v3:
time: 58.1 us; the launch traced here: 57.9 us
  Pallas kernels  56 us (96%)
  between operations  1.93 us (3%)
    pallas_call x1, Pallas kernels, body(): pl.pallas_call(functools.partial(kernel, n, inside), out_shape=shapes, in...  53.4 us
    pallas_call x1, Pallas kernels, body(): pl.pallas_call(finish, out_shape=[jax.ShapeDtypeStruct(whole.shape, whole...  2.63 us

profile of v3, /device:TPU:0, one launch (start us, length us, event | category | flops | bytes accessed | tf_op | source)
XLA Modules:
  0.0 57.9 jit_solution(6549003627580578149)
XLA Ops:
  1.9 53.4 %mesh_step.1 = (bf16[256,512]{1,0:T(8,128)(2,1)}, bf16[256,512]{1,0:T(8,128)(2,1)}, f32[64,1024]{1,0:T(8,128)}, f32[8,128]{1,0:T(8,128)}, f32[64,512]{1,0:T(8,128)}, /*index=5*/f32[32,512]{1,0:T(8,128)}) custom-call(bf16[256,512]{1,0:T(8,128)(2,1)} %refs_0_.1, s32[1]{0:T(128)S(6)} %copy.18.refs_1_, s32[1,1024]{1,0:T(1,128)} %bitcast.4, s32[1,1024]{1,0:T(1,128)} %bitcast.5, ...), custom_call_target="tpu_custom_call" | custom-call | tf_op jit(solution)/shard_map/mesh_step/pallas_call | solution.py:513
  55.3 2.6 %place_results.1 = (bf16[256,512]{1,0:T(8,128)(2,1)}, bf16[256,512]{1,0:T(8,128)(2,1)}, f32[64,1024]{1,0:T(8,128)}, f32[64,512]{1,0:T(8,128)}, f32[32,512]{1,0:T(8,128)}, /*index=5*/f32[64]{0:T(128)}) custom-call(f32[8,128]{1,0:T(8,128)} %get-tuple-element.18.g_bias, bf16[256,512]{1,0:T(8,128)(2,1)} %get-tuple-element.19.refs_0_, ...), custom_call_target="tpu_custom_call" | custom-call | tf_op jit(solution)/shard_map/place_results/pallas_call | solution.py:539
